TPU v7x, 1024 devices: a whole 4x8x16 slice. The times are simulated.
1024 devices in a mesh: dp: 4 (over y_lo), expert: 32 (over z, core), shard: 8 (over x, y_hi).
Axes of the slice: x: 4, y: 8 (y_hi: 2, y_lo: 4; y = y_hi * 4 + y_lo), z: 16, core: 2. Of those that a mesh axis runs over, the one named last changes fastest.
Arguments:
- tokens: bfloat16 [32768, 2048], P(('dp', 'expert'), 'shard'), may hold values from -6 to 6
- out_grad: bfloat16 [32768, 2048], P(('dp', 'expert'), 'shard'), may hold values from -6 to 6
- expert_ids: int32 [32768, 1], P(('dp', 'expert')), may hold values from 0 to 31; in each aligned block of 256 rows (0 to 255, 256 to 511, ...) at most 16 rows name the same one
- combine: float32 [32768, 1], P(('dp', 'expert')), may hold values from 0.05 to 0.45
- old_place: int32 [32], replicated, may hold values from 0 to 31, as said below
- new_place: int32 [32], replicated, may hold values from 0 to 31
- master: float32 [32, 3, 384, 2048], P('expert', None, 'shard', 'dp'), may hold values from -0.125 to 0.125
- moment_one: float32 [32, 3, 384, 2048], P('expert', None, 'shard', 'dp'), may hold values from -4 to 4
- moment_two: float32 [32, 3, 384, 2048], P('expert', None, 'shard', 'dp'), may hold values from 0.5 to 8
Outputs:
- token_grad: bfloat16 [32768, 2048], P(('dp', 'expert'), 'shard')
- master_out: float32 [32, 3, 384, 2048], P('expert', None, 'shard', 'dp')
- first_out: float32 [32, 3, 384, 2048], P('expert', None, 'shard', 'dp')
- second_out: float32 [32, 3, 384, 2048], P('expert', None, 'shard', 'dp')
Inputs may be any that keep to these rules, and one draw needn't show every extreme that they name: old_place is a permutation of the owners; new_place equals old_place except in exactly 8 entries, which hold a cyclic rotation of those entries' owners. `expert_ids`: each token names exactly one expert of the window; among the 256 rows of one block no expert is named more than 16 times, a bound that some block reaches.
All inputs are finite; a program needn't handle non-finite values.
Results may differ from a plain program's by a relative error of at most 0.012.
Values may be sent and summed in bfloat16 or wider, within the bound.
A program may use at most 32 MiB of HBM per device.

v0:
```python
import jax
import jax.numpy as jnp
from jax import lax
from jax.sharding import PartitionSpec as P

beta_first = 0.9
beta_second = 0.95
adam_epsilon = 1e-08
learn_rate = 0.001
weight_decay = 0.1
bias_first = 1.0 - beta_first**10
bias_second = 1.0 - beta_second**10


def sent_together(arrays, axis, split_dim, concat_dim, along):
    widths = [a.shape[along] for a in arrays]
    both = jnp.concatenate(arrays, axis=along)
    filled = lax.all_to_all(both, axis, split_axis=split_dim, concat_axis=concat_dim, tiled=True)
    return tuple(jnp.split(filled, [sum(widths[:k]) for k in range(1, len(widths))], axis=along))


def in_one_piece(arrays, axis, dim, along):
    both = jnp.concatenate(arrays, axis=along)
    filled, at, done = (lax.all_gather(both, axis, axis=dim, tiled=True), 0, [])
    for a in arrays:
        done.append(lax.slice_in_dim(filled, at, at + a.shape[along], axis=along))
        at += a.shape[along]
    return tuple(done)


def laid_out(blocks, dim):
    shape = list(blocks.shape[1:])
    shape[dim] *= blocks.shape[0]
    return jnp.moveaxis(blocks, 0, dim).reshape(shape)


def copy_for_each(x, axis):
    copies = jnp.broadcast_to(x, (lax.axis_size(axis), *x.shape))
    return lax.all_to_all(copies, axis, split_axis=0, concat_axis=0, tiled=True)


def collect(x, axis, dim):
    return laid_out(copy_for_each(x, axis), dim)


def cut_along(x, dim, devices):
    shape = x.shape
    blocks = x.reshape(*shape[:dim], devices, shape[dim] // devices, *shape[dim + 1 :])
    return jnp.moveaxis(blocks, dim, 0)


def summed_on_arrival(x, axis, dim):
    devices = lax.axis_size(axis)
    blocks = lax.all_to_all(cut_along(x, dim, devices), axis, 0, 0, tiled=True)
    return jnp.sum(blocks.astype(jnp.float32), axis=0)


def adamw_step(master, moment_one, moment_two, gradient):
    first_out = beta_first * moment_one + (1.0 - beta_first) * gradient
    second_out = beta_second * moment_two + (1.0 - beta_second) * gradient * gradient
    update = first_out / bias_first / (jnp.sqrt(second_out / bias_second) + adam_epsilon)
    master_out = master - learn_rate * (update + weight_decay * master)
    return (master_out, first_out, second_out)


def on_device(
    tokens, out_grad, expert_ids, combine, old_place, new_place, master, moment_one, moment_two
):
    owner_count = lax.axis_size("expert")
    shard_count = lax.axis_size("shard")
    owners = jnp.arange(owner_count, dtype=jnp.int32)
    holds = (new_place[:, None] == owners[None, :]).astype(jnp.int32)
    source_owner = jnp.sum(old_place[:, None] * holds, axis=0)
    tok_rows, column = tokens.shape
    model_width = column * shard_count
    top_width = expert_ids.shape[1]
    assign = tok_rows * top_width
    capacity = 2 * tok_rows * top_width // owner_count
    slots_all = owner_count * capacity
    flat_ids = expert_ids.reshape(assign)
    onehot = (flat_ids[:, None] == owners[None, :]).astype(jnp.int32)
    earlier = jnp.cumsum(onehot, axis=0) - onehot
    slot = jnp.sum(earlier * onehot, axis=1)
    target = jnp.sum(onehot * new_place[None, :], axis=1)
    position = target * capacity + slot
    slot_ids = jnp.arange(slots_all, dtype=jnp.int32)
    match = position[None, :] == slot_ids[:, None]
    select = jnp.sum(match.reshape(slots_all, tok_rows, top_width).astype(jnp.float32), axis=2)
    slot_scale = jnp.sum(jnp.where(match, combine.reshape(1, assign), 0.0), axis=1)
    select_half = select.astype(jnp.bfloat16)
    rows_x = jnp.dot(select_half, tokens, preferred_element_type=jnp.float32).astype(jnp.bfloat16)
    rows_out = jnp.dot(select_half, out_grad, preferred_element_type=jnp.float32)
    rows_dy = (slot_scale[:, None] * rows_out).astype(jnp.bfloat16)
    arrived_x, arrived_dy = sent_together(
        (
            rows_x.reshape(owner_count, capacity, column),
            rows_dy.reshape(owner_count, capacity, column),
        ),
        "expert",
        0,
        0,
        1,
    )
    whole_x, whole_dy = in_one_piece((arrived_x, arrived_dy), "shard", 2, 0)
    piece_count = master.size // owner_count
    parked_master, parked_one, parked_two = tuple(
        (
            part.astype(jnp.float32)
            for part in sent_together(
                (
                    master.reshape(owner_count, piece_count).astype(jnp.bfloat16),
                    moment_one.reshape(owner_count, piece_count).astype(jnp.bfloat16),
                    moment_two.reshape(owner_count, piece_count).astype(jnp.bfloat16),
                ),
                "expert",
                0,
                0,
                1,
            )
        )
    )
    onward_master = jnp.take(parked_master, source_owner, axis=0)
    onward_one = jnp.take(parked_one, source_owner, axis=0)
    onward_two = jnp.take(parked_two, source_owner, axis=0)
    landed_master, landed_one, landed_two = (
        lax.all_to_all(
            onward_master.astype(jnp.bfloat16), "expert", split_axis=0, concat_axis=0, tiled=True
        ).astype(onward_master.dtype),
        lax.all_to_all(
            onward_one.astype(jnp.bfloat16), "expert", split_axis=0, concat_axis=0, tiled=True
        ).astype(onward_one.dtype),
        lax.all_to_all(
            onward_two.astype(jnp.bfloat16), "expert", split_axis=0, concat_axis=0, tiled=True
        ).astype(onward_two.dtype),
    )
    moved_master = landed_master.reshape(master.shape)
    moved_one = landed_one.reshape(master.shape)
    moved_two = landed_two.reshape(master.shape)
    full_weight = collect(moved_master.astype(jnp.bfloat16), "dp", 3)[0]
    rows_in = whole_x.reshape(slots_all, model_width)
    rows_grad = whole_dy.reshape(slots_all, model_width)
    gate_up = jnp.einsum(
        "rd,gfd->grf", rows_in, full_weight[:2], preferred_element_type=jnp.float32
    )
    gate_pre = gate_up[0]
    up_pre = gate_up[1]
    sigma = jax.nn.sigmoid(gate_pre)
    active = gate_pre * sigma
    hidden = (active * up_pre).astype(jnp.bfloat16)
    grad_hidden = jnp.einsum(
        "rd,fd->rf", rows_grad, full_weight[2], preferred_element_type=jnp.float32
    )
    grad_up = (grad_hidden * active).astype(jnp.bfloat16)
    grad_gate = (grad_hidden * up_pre * sigma * (1.0 + gate_pre * (1.0 - sigma))).astype(
        jnp.bfloat16
    )
    partial_value = jnp.dot(
        grad_gate, full_weight[0], preferred_element_type=jnp.float32
    ) + jnp.dot(grad_up, full_weight[1], preferred_element_type=jnp.float32)
    weight_grad = jnp.stack(
        [
            jnp.einsum("rf,rd->fd", grad_gate, rows_in, preferred_element_type=jnp.float32),
            jnp.einsum("rf,rd->fd", grad_up, rows_in, preferred_element_type=jnp.float32),
            jnp.einsum("rf,rd->fd", hidden, rows_grad, preferred_element_type=jnp.float32),
        ],
        axis=0,
    )
    gradient = summed_on_arrival(weight_grad.astype(jnp.bfloat16), "dp", 2)
    master_out, first_out, second_out = adamw_step(
        moved_master, moved_one, moved_two, gradient[None]
    )
    summed = summed_on_arrival(partial_value.astype(jnp.bfloat16), "shard", 1)
    returned = lax.all_to_all(
        summed.reshape(owner_count, capacity, column).astype(jnp.bfloat16),
        "expert",
        split_axis=0,
        concat_axis=0,
        tiled=True,
    ).astype(jnp.float32)
    row_grad = returned.reshape(slots_all, column)
    token_grad = jnp.dot(select.T, row_grad, precision=lax.Precision.HIGHEST)
    return (token_grad.astype(jnp.bfloat16), master_out, first_out, second_out)


def solution(mesh):
    in_specs = (
        P(("dp", "expert"), "shard"),
        P(("dp", "expert"), "shard"),
        P(("dp", "expert"), None),
        P(("dp", "expert"), None),
        P(),
        P(),
        P("expert", None, "shard", "dp"),
        P("expert", None, "shard", "dp"),
        P("expert", None, "shard", "dp"),
    )
    out_specs = (
        P(("dp", "expert"), "shard"),
        P("expert", None, "shard", "dp"),
        P("expert", None, "shard", "dp"),
        P("expert", None, "shard", "dp"),
    )
    return jax.shard_map(
        on_device, mesh=mesh, in_specs=in_specs, out_specs=out_specs, check_vma=False
    )
```

profile of v0, /device:TPU:1, one launch (start us, length us, event | category | flops | bytes accessed | tf_op | source)
XLA Modules:
  0.0 342.7 jit_solution(11655759900743560794)
XLA Ops:
  10.6 1.1 fusion
  11.9 53.9 %all_to_all.67 = bf16[32,32,256]{2,1,0:T(8,128)(2,1)S(1)} all-to-all(bf16[32,32,256]{2,1,0:T(8,128)(2,1)S(1)} %pad_maximum_fusion), channel_id=1, replica_groups=mesh['dp'=4,'expert'=32,'shard'=8] {'expert'}, dimensions={0} | all-to-all | bytes 1048576 | tf_op jit(solution)/shard_map/all_to_all | solution.py:18
  69.7 4.0 %all-to-all-start.1 = ((bf16[32,2,3456]{2,1,0:T(2,128)(2,1)}), bf16[32,2,3456]{2,1,0:T(2,128)(2,1)S(1)}, u32[]{:S(2)}, u32[]{:S(2)}) async-start(bf16[32,2,3456]{2,1,0:T(2,128)(2,1)} %reshape.351), calls=%async_computation.1 | async-start | bytes 884736 | tf_op jit(solution)/shard_map/all_to_all | solution.py:18
  73.9 29.9 %all-to-all-done.1 = bf16[32,2,3456]{2,1,0:T(2,128)(2,1)S(1)} async-done(((bf16[32,2,3456]{2,1,0:T(2,128)(2,1)}), bf16[32,2,3456]{2,1,0:T(2,128)(2,1)S(1)}, u32[]{:S(2)}, u32[]{:S(2)}) %all-to-all-start.1) | async-done | bytes 442400 | tf_op jit(solution)/shard_map/all_to_all | solution.py:18
  107.2 20.3 %all_to_all.68 = bf16[32,2,1152]{2,1,0:T(2,128)(2,1)S(1)} all-to-all(bf16[32,2,1152]{2,1,0:T(2,128)(2,1)S(1)} %reshape.353), channel_id=1, replica_groups=mesh['dp'=4,'expert'=32,'shard'=8] {'expert'}, dimensions={0} | all-to-all | bytes 294912 | tf_op jit(solution)/shard_map/all_to_all | solution.py:126
  129.5 4.6 %all-to-all-start.3 = ((bf16[4,1,3,48,512]{4,3,2,1,0:T(8,128)(2,1)}), bf16[4,1,3,48,512]{4,3,2,1,0:T(8,128)(2,1)S(1)}, u32[]{:S(2)}, u32[]{:S(2)}) async-start(bf16[4,1,3,48,512]{4,3,2,1,0:T(8,128)(2,1)} %broadcast_in_dim.38), calls=%async_computation.3 | async-start | bytes 1179648 | tf_op jit(solution)/shard_map/all_to_all | solution.py:39
  136.9 42.4 %all-to-all-done.3 = bf16[4,1,3,48,512]{4,3,2,1,0:T(8,128)(2,1)S(1)} async-done(((bf16[4,1,3,48,512]{4,3,2,1,0:T(8,128)(2,1)}), bf16[4,1,3,48,512]{4,3,2,1,0:T(8,128)(2,1)S(1)}, u32[]{:S(2)}, u32[]{:S(2)}) %all-to-all-start.3) | async-done | bytes 589856 | tf_op jit(solution)/shard_map/all_to_all | solution.py:39
  179.3 13.5 %all-to-all-start.6 = ((bf16[32,2,1152]{2,1,0:T(2,128)(2,1)}), bf16[32,2,1152]{2,1,0:T(2,128)(2,1)S(1)}, u32[]{:S(2)}, u32[]{:S(2)}) async-start(bf16[32,2,1152]{2,1,0:T(2,128)(2,1)} %reshape.357), calls=%async_computation.6 | async-start | bytes 294912 | tf_op jit(solution)/shard_map/all_to_all | solution.py:129
  194.8 2.6 fusion.33
  200.2 9.1 %all-to-all-done.6 = bf16[32,2,1152]{2,1,0:T(2,128)(2,1)S(1)} async-done(((bf16[32,2,1152]{2,1,0:T(2,128)(2,1)}), bf16[32,2,1152]{2,1,0:T(2,128)(2,1)S(1)}, u32[]{:S(2)}, u32[]{:S(2)}) %all-to-all-start.6) | async-done | bytes 147488 | tf_op jit(solution)/shard_map/all_to_all | solution.py:129
  209.3 5.2 %all-to-all-start.8 = ((bf16[32,2,1152]{2,1,0:T(2,128)(2,1)}), bf16[32,2,1152]{2,1,0:T(2,128)(2,1)S(1)}, u32[]{:S(2)}, u32[]{:S(2)}) async-start(bf16[32,2,1152]{2,1,0:T(2,128)(2,1)} %reshape.355), calls=%async_computation.8 | async-start | bytes 294912 | tf_op jit(solution)/shard_map/all_to_all | solution.py:132
  215.9 1.4 copy.68
  217.4 14.0 %all-to-all-done.8 = bf16[32,2,1152]{2,1,0:T(2,128)(2,1)S(1)} async-done(((bf16[32,2,1152]{2,1,0:T(2,128)(2,1)}), bf16[32,2,1152]{2,1,0:T(2,128)(2,1)S(1)}, u32[]{:S(2)}, u32[]{:S(2)}) %all-to-all-start.8) | async-done | bytes 147488 | tf_op jit(solution)/shard_map/all_to_all | solution.py:132
  231.4 6.3 %all-to-all-start.4 = ((bf16[8,512,256]{2,1,0:T(8,128)(2,1)}), bf16[8,512,256]{2,1,0:T(8,128)(2,1)}, u32[]{:S(2)}, u32[]{:S(2)}) async-start(bf16[8,512,256]{2,1,0:T(8,128)(2,1)} %bitcast.142), calls=%async_computation.4 | async-start | bytes 4194304 | tf_op jit(solution)/shard_map/all_to_all | solution.py:54
  237.7 2.5 copy.55
  240.2 2.9 copy.58
  246.4 40.9 %all-to-all-done.4 = bf16[8,512,256]{2,1,0:T(8,128)(2,1)} async-done(((bf16[8,512,256]{2,1,0:T(8,128)(2,1)}), bf16[8,512,256]{2,1,0:T(8,128)(2,1)}, u32[]{:S(2)}, u32[]{:S(2)}) %all-to-all-start.4) | async-done | bytes 2097184 | tf_op jit(solution)/shard_map/all_to_all | solution.py:54
  287.3 4.2 %all-to-all-start.7 = ((bf16[4,3,48,512]{3,2,1,0:T(8,128)(2,1)}), bf16[4,3,48,512]{3,2,1,0:T(8,128)(2,1)S(1)}, u32[]{:S(2)}, u32[]{:S(2)}) async-start(bf16[4,3,48,512]{3,2,1,0:T(8,128)(2,1)} %copy.56), calls=%async_computation.7 | async-start | bytes 1179648 | tf_op jit(solution)/shard_map/all_to_all | solution.py:54
  291.5 2.7 reduce_sum.67
  294.2 11.8 %all-to-all-done.7 = bf16[4,3,48,512]{3,2,1,0:T(8,128)(2,1)S(1)} async-done(((bf16[4,3,48,512]{3,2,1,0:T(8,128)(2,1)}), bf16[4,3,48,512]{3,2,1,0:T(8,128)(2,1)S(1)}, u32[]{:S(2)}, u32[]{:S(2)}) %all-to-all-start.7) | async-done | bytes 589856 | tf_op jit(solution)/shard_map/all_to_all | solution.py:54
  305.9 6.9 %all-to-all-start.5 = ((bf16[32,16,256]{2,1,0:T(8,128)(2,1)}), bf16[32,16,256]{2,1,0:T(8,128)(2,1)S(1)}, u32[]{:S(2)}, u32[]{:S(2)}) async-start(bf16[32,16,256]{2,1,0:T(8,128)(2,1)} %bitcast.17), calls=%async_computation.5 | async-start | bytes 524288 | tf_op jit(solution)/shard_map/all_to_all | solution.py:173
  316.1 1.0 multiply_subtract_fusion
  317.1 17.7 %all-to-all-done.5 = bf16[32,16,256]{2,1,0:T(8,128)(2,1)S(1)} async-done(((bf16[32,16,256]{2,1,0:T(8,128)(2,1)}), bf16[32,16,256]{2,1,0:T(8,128)(2,1)S(1)}, u32[]{:S(2)}, u32[]{:S(2)}) %all-to-all-start.5) | async-done | bytes 262176 | tf_op jit(solution)/shard_map/all_to_all | solution.py:173
  334.9 1.0 convolution_convert_fusion.4
  (100 shorter events, 28.1 us)
Async XLA Ops:
  7.2 3.2 copy-start
  7.2 187.6 %all-gather.2.cloned.1.call-start = ((), (), s32[]{:S(2)}) async-start(), calls=%async_computation.9 | async-start | bytes 4718592 | tf_op jit(solution)/shard_map/all_gather | solution.py:24
  11.9 54.8 %copy-start.7 = (f32[1,3,48,512]{3,2,1,0:T(8,128)S(1)}, f32[1,3,48,512]{3,2,1,0:T(8,128)}, u32[]{:S(2)}) copy-start(f32[1,3,48,512]{3,2,1,0:T(8,128)} %param.17) | copy-start | bytes 884740
  11.9 55.0 %copy-start.8 = (f32[1,3,48,512]{3,2,1,0:T(8,128)S(1)}, f32[1,3,48,512]{3,2,1,0:T(8,128)}, u32[]{:S(2)}) copy-start(f32[1,3,48,512]{3,2,1,0:T(8,128)} %param.18) | copy-start | bytes 884740
  65.7 1.4 copy-start.9
  67.2 6.6 %copy-start.11 = (s32[32]{0:T(128)S(1)}, s32[32]{0:T(128)}, u32[]{:S(2)}) copy-start(s32[32]{0:T(128)} %param.16) | copy-start | bytes 388
  67.2 6.6 %copy-start.12 = (s32[32]{0:T(128)S(1)}, s32[32]{0:T(128)}, u32[]{:S(2)}) copy-start(s32[32]{0:T(128)} %param.15) | copy-start | bytes 388
  69.7 34.1 %all-to-all-start.1 = ((bf16[32,2,3456]{2,1,0:T(2,128)(2,1)}), bf16[32,2,3456]{2,1,0:T(2,128)(2,1)S(1)}, u32[]{:S(2)}, u32[]{:S(2)}) async-start(bf16[32,2,3456]{2,1,0:T(2,128)(2,1)} %reshape.351), calls=%async_computation.1 | async-start | bytes 884736 | tf_op jit(solution)/shard_map/all_to_all | solution.py:18
  129.5 49.7 %all-to-all-start.3 = ((bf16[4,1,3,48,512]{4,3,2,1,0:T(8,128)(2,1)}), bf16[4,1,3,48,512]{4,3,2,1,0:T(8,128)(2,1)S(1)}, u32[]{:S(2)}, u32[]{:S(2)}) async-start(bf16[4,1,3,48,512]{4,3,2,1,0:T(8,128)(2,1)} %broadcast_in_dim.38), calls=%async_computation.3 | async-start | bytes 1179648 | tf_op jit(solution)/shard_map/all_to_all | solution.py:39
  179.3 30.0 %all-to-all-start.6 = ((bf16[32,2,1152]{2,1,0:T(2,128)(2,1)}), bf16[32,2,1152]{2,1,0:T(2,128)(2,1)S(1)}, u32[]{:S(2)}, u32[]{:S(2)}) async-start(bf16[32,2,1152]{2,1,0:T(2,128)(2,1)} %reshape.357), calls=%async_computation.6 | async-start | bytes 294912 | tf_op jit(solution)/shard_map/all_to_all | solution.py:129
  197.4 1.3 copy-start.3
  197.4 2.8 copy-start.1
  197.4 2.0 copy-start.10
  198.2 1.2 copy-start.5
  209.3 22.1 %all-to-all-start.8 = ((bf16[32,2,1152]{2,1,0:T(2,128)(2,1)}), bf16[32,2,1152]{2,1,0:T(2,128)(2,1)S(1)}, u32[]{:S(2)}, u32[]{:S(2)}) async-start(bf16[32,2,1152]{2,1,0:T(2,128)(2,1)} %reshape.355), calls=%async_computation.8 | async-start | bytes 294912 | tf_op jit(solution)/shard_map/all_to_all | solution.py:132
  231.4 6.3 %copy-start.4 = (bf16[32,16,2048]{2,1,0:T(8,128)(2,1)S(1)}, bf16[32,16,2048]{2,1,0:T(8,128)(2,1)}, u32[]{:S(2)}) copy-start(bf16[32,16,2048]{2,1,0:T(8,128)(2,1)} %copy-done.3) | copy-start | bytes 6291460
  231.4 55.9 %all-to-all-start.4 = ((bf16[8,512,256]{2,1,0:T(8,128)(2,1)}), bf16[8,512,256]{2,1,0:T(8,128)(2,1)}, u32[]{:S(2)}, u32[]{:S(2)}) async-start(bf16[8,512,256]{2,1,0:T(8,128)(2,1)} %bitcast.142), calls=%async_computation.4 | async-start | bytes 4194304 | tf_op jit(solution)/shard_map/all_to_all | solution.py:54
  243.1 1.6 copy-start.2
  243.1 1.6 copy-start.6
  287.3 18.6 %all-to-all-start.7 = ((bf16[4,3,48,512]{3,2,1,0:T(8,128)(2,1)}), bf16[4,3,48,512]{3,2,1,0:T(8,128)(2,1)S(1)}, u32[]{:S(2)}, u32[]{:S(2)}) async-start(bf16[4,3,48,512]{3,2,1,0:T(8,128)(2,1)} %copy.56), calls=%async_computation.7 | async-start | bytes 1179648 | tf_op jit(solution)/shard_map/all_to_all | solution.py:54
  305.9 28.9 %all-to-all-start.5 = ((bf16[32,16,256]{2,1,0:T(8,128)(2,1)}), bf16[32,16,256]{2,1,0:T(8,128)(2,1)S(1)}, u32[]{:S(2)}, u32[]{:S(2)}) async-start(bf16[32,16,256]{2,1,0:T(8,128)(2,1)} %bitcast.17), calls=%async_computation.5 | async-start | bytes 524288 | tf_op jit(solution)/shard_map/all_to_all | solution.py:173
Sparse Core Ops, SparseCore 0:
  66.8 127.2 all-gather.1
where the time goes:
time: 344 us; the launch traced here: 343 us
  waiting for transfers between devices  166 us (48%)
  blocking collectives  74.2 us (22%)
  starting transfers between devices  44.8 us (13%)
  local copies, waits for them, and re-layouts  21.2 us (6%)
  between operations  14.6 us (4%)
  other arithmetic  14.5 us (4%)
  matrix products  7.55 us (2%)
    all_to_all x1, blocking collectives, sent_together(): lax.all_to_all(both, axis, split_axis=split_dim, concat_axis=concat_dim,...  53.9 us
    all_to_all x2, waiting for transfers between devices, summed_on_arrival(): blocks = lax.all_to_all(cut_along(x, dim, devices), axis, 0, 0, tiled=True)  52.7 us
    all_to_all x1, waiting for transfers between devices, copy_for_each(): return lax.all_to_all(copies, axis, split_axis=0, concat_axis=0, tiled=True)  42.4 us
    all_to_all x1, waiting for transfers between devices, sent_together(): lax.all_to_all(both, axis, split_axis=split_dim, concat_axis=concat_dim,...  29.9 us
    all_to_all x1, blocking collectives, on_device(): lax.all_to_all(onward_master.astype(jnp.bfloat16), 'expert', split_axis=0...  20.3 us
    all_to_all x1, waiting for transfers between devices, on_device(): lax.all_to_all(summed.reshape(owner_count, capacity, column).astype(jnp.b...  17.7 us
    all_to_all x1, waiting for transfers between devices, on_device(): lax.all_to_all(onward_two.astype(jnp.bfloat16), 'expert', split_axis=0, c...  14 us
    all_to_all x1, starting transfers between devices, on_device(): lax.all_to_all(onward_one.astype(jnp.bfloat16), 'expert', split_axis=0, c...  13.5 us
  transfers between devices with their start and end apart: 8, of which 7 were waited for; matrix products, arithmetic and copies ran while one was open for 10% of the time, Pallas kernels for 0%

commit v1 on v0

v1 whole, which is shorter than its diff:
```python
import functools

import jax
import jax.numpy as jnp
from jax import lax
from jax.experimental import pallas as pl
from jax.experimental.pallas import tpu as pltpu
from jax.sharding import PartitionSpec as P

MESH = pl.DeviceIdType.MESH
bf16 = jnp.bfloat16
f32 = jnp.float32

beta_first = 0.9
beta_second = 0.95
adam_epsilon = 1e-08
learn_rate = 0.001
weight_decay = 0.1
bias_first = 1.0 - beta_first**10
bias_second = 1.0 - beta_second**10

CHUNKS = 4
CAP = 16
PARKS = ((0, 0), (0, 1), (2, 0))


def same_bytes(ref, sem):
    return pltpu.make_async_copy(ref, ref, sem)


def adamw_step(master, moment_one, moment_two, gradient):
    first_out = beta_first * moment_one + (1.0 - beta_first) * gradient
    second_out = beta_second * moment_two + (1.0 - beta_second) * gradient * gradient
    update = first_out / bias_first / (jnp.sqrt(second_out / bias_second) + adam_epsilon)
    master_out = master - learn_rate * (update + weight_decay * master)
    return master_out, first_out, second_out


def kernel(
    source_ref, place_ref, ids_ref, combine_ref, tokens_ref, out_grad_ref,
    master_ref, one_ref, two_ref,
    token_grad_ref, master_out_ref, first_out_ref, second_out_ref,
    match, rows_out, rows_in, states, parked, onward, moved,
    weight, partial, rs, yb, yr, act, row_grad, returned, wgrad, grads,
    send_sem, rows_sem, park_sem, moved_sem, weight_sem, rs_sem, y_sem, ag_sem, ret_sem, grad_sem,
):
    p = lax.axis_index("dp")
    me = lax.axis_index("expert")
    s = lax.axis_index("shard")
    z, core = me // 2, me % 2
    x, yh = s // 2, s % 2
    n_owner = 32
    n_rows = n_owner * CAP
    chunk_rows = n_rows // CHUNKS
    block_rows = chunk_rows // 4
    width = tokens_ref.shape[1]
    ff = weight.shape[1]
    part_ff = ff // 8

    barrier = pltpu.get_barrier_semaphore()

    def greet(device):
        pl.semaphore_signal(barrier, inc=1, device_id=device, device_id_type=MESH)

    def greet_owner(i, c):
        greet({"expert": (me + i) % n_owner})
        return c

    lax.fori_loop(1, n_owner, greet_owner, 0)
    for j in (1, 2, 3):
        greet({"shard": ((x + j) % 4) * 2 + yh})
    greet({"shard": x * 2 + 1 - yh})
    diagonal = x == p

    def greet_spread(i, c):
        h, q = i // 4, i % 4

        @pl.when(jnp.logical_or(q != p, p * 2 + h != s))
        def _():
            greet({"dp": q, "shard": p * 2 + h})

        @pl.when(jnp.logical_or(x != p, i != s))
        def _():
            greet({"dp": x, "shard": i})

        return c

    lax.fori_loop(0, 8, greet_spread, 0)
    states[0] = master_ref[0].astype(bf16)
    pl.semaphore_wait(barrier, jnp.where(diagonal, 49, 51))

    def park_device(a, k):
        shift, c = PARKS[a]
        return 2 * ((k + k // 3 + shift) % 16) + c

    def is_park(a):
        shift, c = PARKS[a]
        zz = (z + 16 - shift) % 16
        return jnp.logical_and(core == c, zz % 4 != 3), zz - zz // 4

    def park(a):
        def step(k, c):
            g, lane = k // 4, pl.multiple_of((k % 4) * 128, 128)
            dest = park_device(a, k)
            src = states.at[a, g, :, pl.ds(lane, 128)]

            @pl.when(dest != me)
            def _():
                pltpu.make_async_remote_copy(
                    src_ref=src, dst_ref=parked.at[a, me], send_sem=send_sem.at[a],
                    recv_sem=park_sem.at[a], device_id={"expert": dest}, device_id_type=MESH,
                ).start()

            @pl.when(dest == me)
            def _():
                pltpu.make_async_copy(src, parked.at[a, me], park_sem.at[a]).start()

            return c

        lax.fori_loop(0, 12, step, 0)

    def send_on(a):
        mine, k = is_park(a)
        g, lane = k // 4, pl.multiple_of((k % 4) * 128, 128)

        @pl.when(mine)
        def _():
            same_bytes(parked.at[a], park_sem.at[a]).wait()

            def step(i, c):
                o = (me + i) % n_owner
                onward[a, o] = parked[a, source_ref[o]]
                dst = moved.at[a, g, :, pl.ds(lane, 128)]

                @pl.when(i != 0)
                def _():
                    pltpu.make_async_remote_copy(
                        src_ref=onward.at[a, o], dst_ref=dst, send_sem=send_sem.at[3 + a],
                        recv_sem=moved_sem.at[a], device_id={"expert": o}, device_id_type=MESH,
                    ).start()

                @pl.when(i == 0)
                def _():
                    pltpu.make_async_copy(onward.at[a, o], dst, moved_sem.at[a]).start()

                return c

            lax.fori_loop(0, n_owner, step, 0)

    def states_sent(a):
        mine, _ = is_park(a)

        @pl.when(mine)
        def _():
            same_bytes(onward.at[a, pl.ds(0, 11)], send_sem.at[a]).wait()
            same_bytes(onward.at[a, pl.ds(0, 31)], send_sem.at[3 + a]).wait()

        @pl.when(jnp.logical_not(mine))
        def _():
            same_bytes(onward.at[a, pl.ds(0, 12)], send_sem.at[a]).wait()

    park(0)

    tok = tokens_ref.shape[0]
    eye = lax.broadcasted_iota(jnp.int32, (n_owner, n_owner), 0) == lax.broadcasted_iota(
        jnp.int32, (n_owner, n_owner), 1
    )
    place = jnp.sum(jnp.where(eye, place_ref[...].astype(f32), 0.0), axis=1, keepdims=True)
    onehot = jnp.where(
        lax.broadcasted_iota(jnp.int32, (n_owner, tok), 0) == ids_ref[...], 1.0, 0.0
    )
    before = jnp.where(
        lax.broadcasted_iota(jnp.int32, (tok, tok), 0) < lax.broadcasted_iota(jnp.int32, (tok, tok), 1),
        1.0, 0.0,
    ).astype(bf16)
    earlier = jnp.dot(onehot.astype(bf16), before, preferred_element_type=f32)
    position = jnp.sum(onehot * (earlier + place * float(CAP)), axis=0, keepdims=True)
    chosen = lax.broadcasted_iota(jnp.int32, (n_rows, tok), 0).astype(f32) == position
    match[...] = jnp.where(chosen, 1.0, 0.0).astype(bf16)
    scale = jnp.sum(jnp.where(chosen, combine_ref[...], 0.0), axis=1, keepdims=True)
    rows_out[:, :width] = jnp.dot(match[...], tokens_ref[...], preferred_element_type=f32).astype(bf16)
    rows_out[:, width:] = (
        scale * jnp.dot(match[...], out_grad_ref[...], preferred_element_type=f32)
    ).astype(bf16)

    send_on(0)

    def dz_of(rank):
        return jnp.where(rank % 2 == 1, (rank + 1) // 2, (16 - rank // 2) % 16)

    def dispatch(i, c):
        rank, to_core = i // 2, i % 2
        dest = ((z + 16 - dz_of(rank)) % 16) * 2 + to_core
        src = rows_out.at[pl.ds(pl.multiple_of(dest * CAP, CAP), CAP), :]
        dst = rows_in.at[pl.ds(pl.multiple_of((rank * 2 + core) * CAP, CAP), CAP), :]
        sem = rows_sem.at[rank // (16 // CHUNKS)]

        @pl.when(dest != me)
        def _():
            pltpu.make_async_remote_copy(
                src_ref=src, dst_ref=dst, send_sem=send_sem.at[6], recv_sem=sem,
                device_id={"expert": dest}, device_id_type=MESH,
            ).start()

        @pl.when(dest == me)
        def _():
            pltpu.make_async_copy(src, dst, sem).start()

        return c

    lax.fori_loop(0, n_owner, dispatch, 0)

    same_bytes(moved.at[0], moved_sem.at[0]).wait()

    def spread(i, c):
        h, q = i // 4, i % 4
        src = moved.at[0, :, :, pl.ds(pl.multiple_of(h * width, width), width)]
        dst = weight.at[:, pl.ds(pl.multiple_of(s * part_ff, 16), part_ff), :]
        away = jnp.logical_or(q != p, p * 2 + h != s)

        @pl.when(away)
        def _():
            pltpu.make_async_remote_copy(
                src_ref=src, dst_ref=dst, send_sem=send_sem.at[7], recv_sem=weight_sem,
                device_id={"dp": q, "shard": p * 2 + h}, device_id_type=MESH,
            ).start()

        @pl.when(jnp.logical_not(away))
        def _():
            pltpu.make_async_copy(src, dst, weight_sem).start()

        return c

    lax.fori_loop(0, 8, spread, 0)
    states[1] = one_ref[0].astype(bf16)
    states[2] = two_ref[0].astype(bf16)
    same_bytes(weight, weight_sem).wait()

    def products(c):
        same_bytes(rows_in.at[pl.ds(c * chunk_rows, chunk_rows)], rows_sem.at[c]).wait()
        rows = rows_in[pl.ds(c * chunk_rows, chunk_rows), :]
        nt = (((1,), (1,)), ((), ()))
        here = pl.ds(c * chunk_rows, chunk_rows)
        for g in range(3):
            lhs = rows[:, :width] if g < 2 else rows[:, width:]
            partial[here, g * ff : (g + 1) * ff] = lax.dot_general(
                lhs, weight[g], nt, preferred_element_type=f32
            ).astype(bf16)
        for j in (1, 2, 3):
            xx = (x + j) % 4
            pltpu.make_async_remote_copy(
                src_ref=partial.at[pl.ds(pl.multiple_of(c * chunk_rows + xx * block_rows, 16), block_rows), :],
                dst_ref=rs.at[c, j - 1], send_sem=send_sem.at[8], recv_sem=rs_sem.at[c],
                device_id={"shard": xx * 2 + yh}, device_id_type=MESH,
            ).start()

    def own_rows(c):
        return pl.ds(pl.multiple_of(c * chunk_rows + x * block_rows, 16), block_rows)

    def half_sums(c):
        same_bytes(rs.at[c], rs_sem.at[c]).wait()
        total = partial[own_rows(c), :].astype(f32)
        for j in range(3):
            total += rs[c, j].astype(f32)
        yb[c] = total.astype(bf16)
        pltpu.make_async_remote_copy(
            src_ref=yb.at[c], dst_ref=yr.at[c], send_sem=send_sem.at[9], recv_sem=y_sem.at[c],
            device_id={"shard": x * 2 + 1 - yh}, device_id_type=MESH,
        ).start()

    def activations(c):
        same_bytes(yr.at[c], y_sem.at[c]).wait()
        total = yb[c].astype(f32) + yr[c].astype(f32)
        gate, up, grad_hidden = total[:, :ff], total[:, ff : 2 * ff], total[:, 2 * ff :]
        sigma = jax.nn.sigmoid(gate)
        active = gate * sigma
        here = own_rows(c)
        act[here, :ff] = (grad_hidden * up * sigma * (1.0 + gate * (1.0 - sigma))).astype(bf16)
        act[here, ff : 2 * ff] = (grad_hidden * active).astype(bf16)
        act[here, 2 * ff :] = (active * up).astype(bf16)
        for j in (1, 2, 3):
            xx = (x + j) % 4
            pltpu.make_async_remote_copy(
                src_ref=act.at[here, :], dst_ref=act.at[here, :], send_sem=send_sem.at[10],
                recv_sem=ag_sem.at[c], device_id={"shard": xx * 2 + yh}, device_id_type=MESH,
            ).start()

    def gathered(c):
        same_bytes(rs.at[c], ag_sem.at[c]).wait()

    def row_grads(c):
        here = pl.ds(c * chunk_rows, chunk_rows)
        row_grad[here, :] = (
            jnp.dot(act[here, :ff], weight[0], preferred_element_type=f32)
            + jnp.dot(act[here, ff : 2 * ff], weight[1], preferred_element_type=f32)
        ).astype(bf16)

        def give_back(i, carry):
            rank, to_core = i // 2, i % 2
            dest = ((z + dz_of(rank)) % 16) * 2 + to_core
            src = row_grad.at[pl.ds(pl.multiple_of(i * CAP, CAP), CAP), :]
            dst = returned.at[pl.ds(pl.multiple_of(me * CAP, CAP), CAP), :]

            @pl.when(dest != me)
            def _():
                pltpu.make_async_remote_copy(
                    src_ref=src, dst_ref=dst, send_sem=send_sem.at[11], recv_sem=ret_sem,
                    device_id={"expert": dest}, device_id_type=MESH,
                ).start()

            @pl.when(dest == me)
            def _():
                pltpu.make_async_copy(src, dst, ret_sem).start()

            return carry

        lax.fori_loop(c * (n_owner // CHUNKS), (c + 1) * (n_owner // CHUNKS), give_back, 0)

    for step in range(CHUNKS + 2):
        if step < CHUNKS:
            products(step)
        if step == CHUNKS - 1:
            park(1)
            park(2)
        if 0 <= step - 1 < CHUNKS:
            half_sums(step - 1)
        if 0 <= step - 2 < CHUNKS:
            activations(step - 2)
    send_on(1)
    send_on(2)
    for c in range(CHUNKS - 1):
        gathered(c)
        row_grads(c)
    gathered(CHUNKS - 1)

    tn = (((0,), (0,)), ((), ()))
    for g in range(3):
        right = rows_in[:, :width] if g < 2 else rows_in[:, width:]
        wgrad[g] = lax.dot_general(
            act[:, g * ff : (g + 1) * ff], right, tn, preferred_element_type=f32
        ).astype(bf16)

    def to_holder(i, c):
        src = wgrad.at[:, pl.ds(pl.multiple_of(i * part_ff, 16), part_ff), :]
        dst = grads.at[yh * 4 + p]
        away = jnp.logical_or(x != p, i != s)

        @pl.when(away)
        def _():
            pltpu.make_async_remote_copy(
                src_ref=src, dst_ref=dst, send_sem=send_sem.at[12], recv_sem=grad_sem,
                device_id={"dp": x, "shard": i}, device_id_type=MESH,
            ).start()

        @pl.when(jnp.logical_not(away))
        def _():
            pltpu.make_async_copy(src, dst, grad_sem).start()

        return c

    lax.fori_loop(0, 8, to_holder, 0)
    row_grads(CHUNKS - 1)

    same_bytes(returned, ret_sem).wait()
    token_grad_ref[...] = lax.dot_general(
        match[...], returned[...], tn, preferred_element_type=f32
    ).astype(bf16)

    same_bytes(moved.at[1], moved_sem.at[1]).wait()
    same_bytes(moved.at[2], moved_sem.at[2]).wait()
    same_bytes(grads, grad_sem).wait()
    for h in range(2):
        half = slice(h * width, (h + 1) * width)
        for g in range(3):
            gradient = grads[h * 4, g].astype(f32)
            for q in range(1, 4):
                gradient += grads[h * 4 + q, g].astype(f32)
            a, b, d = adamw_step(
                moved[0, g, :, half].astype(f32), moved[1, g, :, half].astype(f32),
                moved[2, g, :, half].astype(f32), gradient,
            )
            master_out_ref[0, g, :, half] = a
            first_out_ref[0, g, :, half] = b
            second_out_ref[0, g, :, half] = d

    for a in range(3):
        states_sent(a)
    same_bytes(rows_out.at[pl.ds(0, 31 * CAP)], send_sem.at[6]).wait()
    for index, buffer in ((7, moved.at[0]), (12, wgrad)):
        @pl.when(diagonal)
        def _(index=index):
            same_bytes(grads.at[pl.ds(0, 7)], send_sem.at[index]).wait()

        @pl.when(jnp.logical_not(diagonal))
        def _(index=index):
            same_bytes(grads, send_sem.at[index]).wait()
    same_bytes(rs, send_sem.at[8]).wait()
    same_bytes(yb, send_sem.at[9]).wait()
    same_bytes(rs, send_sem.at[10]).wait()
    same_bytes(row_grad.at[pl.ds(0, 31 * CAP)], send_sem.at[11]).wait()


def on_device(
    tokens, out_grad, expert_ids, combine, old_place, new_place, master, moment_one, moment_two
):
    n_owner = 32
    owners = jnp.arange(n_owner, dtype=jnp.int32)
    holds = (new_place[:, None] == owners[None, :]).astype(jnp.int32)
    source_owner = jnp.sum(old_place[:, None] * holds, axis=0)
    tok, width = tokens.shape
    _, mats, part_ff, held_width = master.shape
    ff = part_ff * 8
    rows = n_owner * CAP
    block = rows // CHUNKS // 4
    vmem = pl.BlockSpec(memory_space=pltpu.VMEM)
    dma = pltpu.SemaphoreType.DMA
    return pl.pallas_call(
        kernel,
        out_shape=(
            jax.ShapeDtypeStruct(tokens.shape, bf16),
            jax.ShapeDtypeStruct(master.shape, f32),
            jax.ShapeDtypeStruct(master.shape, f32),
            jax.ShapeDtypeStruct(master.shape, f32),
        ),
        in_specs=[pl.BlockSpec(memory_space=pltpu.SMEM)] + [vmem] * 8,
        out_specs=(vmem,) * 4,
        scratch_shapes=[
            pltpu.VMEM((rows, tok), bf16),
            pltpu.VMEM((rows, 2 * width), bf16),
            pltpu.VMEM((rows, 2 * width), bf16),
            pltpu.VMEM((3, mats, part_ff, held_width), bf16),
            pltpu.VMEM((3, n_owner, part_ff, 128), bf16),
            pltpu.VMEM((3, n_owner, part_ff, 128), bf16),
            pltpu.VMEM((3, mats, part_ff, held_width), bf16),
            pltpu.VMEM((mats, ff, width), bf16),
            pltpu.VMEM((rows, 3 * ff), bf16),
            pltpu.VMEM((CHUNKS, 3, block, 3 * ff), bf16),
            pltpu.VMEM((CHUNKS, block, 3 * ff), bf16),
            pltpu.VMEM((CHUNKS, block, 3 * ff), bf16),
            pltpu.VMEM((rows, 3 * ff), bf16),
            pltpu.VMEM((rows, width), bf16),
            pltpu.VMEM((rows, width), bf16),
            pltpu.VMEM((mats, ff, width), bf16),
            pltpu.VMEM((8, mats, part_ff, width), bf16),
            dma((13,)),
            dma((CHUNKS,)),
            dma((3,)),
            dma((3,)),
            dma,
            dma((CHUNKS,)),
            dma((CHUNKS,)),
            dma((CHUNKS,)),
            dma,
            dma,
        ],
        compiler_params=pltpu.CompilerParams(
            collective_id=0, has_side_effects=True, vmem_limit_bytes=40 * 1024 * 1024
        ),
    )(
        source_owner, new_place.reshape(1, n_owner), expert_ids.reshape(1, tok),
        combine.reshape(1, tok), tokens, out_grad, master, moment_one, moment_two,
    )


def solution(mesh):
    in_specs = (
        P(("dp", "expert"), "shard"),
        P(("dp", "expert"), "shard"),
        P(("dp", "expert"), None),
        P(("dp", "expert"), None),
        P(),
        P(),
        P("expert", None, "shard", "dp"),
        P("expert", None, "shard", "dp"),
        P("expert", None, "shard", "dp"),
    )
    out_specs = (
        P(("dp", "expert"), "shard"),
        P("expert", None, "shard", "dp"),
        P("expert", None, "shard", "dp"),
        P("expert", None, "shard", "dp"),
    )
    return jax.shard_map(
        on_device, mesh=mesh, in_specs=in_specs, out_specs=out_specs, check_vma=False
    )
```

time: 344 us -> 146 us (0.42)
  the two profiles are of different devices: /device:TPU:1 before, /device:TPU:61 now
where the time goes in v1:
time: 146 us
  Pallas kernels  136 us (93%)
  local copies, waits for them, and re-layouts  8.72 us (6%)
    pallas_call x1, Pallas kernels, on_device(): pl.pallas_call(kernel, out_shape=(jax.ShapeDtypeStruct(tokens.shape, bf16...  136 us
    unnamed x22, local copies, waits for them, and re-layouts  8.72 us

profile of v1, /device:TPU:61, one launch (start us, length us, event | category | flops | bytes accessed | tf_op | source)
XLA Modules:
  0.0 145.9 jit_solution(1560399264773785079)
XLA Ops:
  0.6 0.0 copy-start.8
  0.6 0.0 copy-start.7
  0.7 0.0 copy-start.6
  0.7 0.6 copy-done.8
  1.3 0.0 copy-done.7
  1.3 0.0 copy-start.5
  1.3 0.1 select_reduce_fusion.source_ref
  1.4 0.0 copy-done.6
  1.4 0.6 copy-done.5
  2.0 0.0 copy-start
  2.0 1.0 copy-done
  2.9 0.0 copy-start.1
  2.9 1.0 copy-done.1
  3.9 0.0 copy-start.2
  3.9 1.0 copy-done.2
  4.9 0.0 copy-start.3
  4.9 0.9 copy-done.3
  5.8 0.0 copy-start.4
  5.8 0.9 copy-done.4
  6.7 136.4 %shard_map.120 = (bf16[256,256]{1,0:T(8,128)(2,1)S(1)}, f32[1,3,48,512]{3,2,1,0:T(8,128)S(1)}, f32[1,3,48,512]{3,2,1,0:T(8,128)S(1)}, f32[1,3,48,512]{3,2,1,0:T(8,128)S(1)}) custom-call(s32[32]{0:T(128)S(1)} %select_reduce_fusion.source_ref, s32[1,32]{1,0:T(1,128)S(1)} %bitcast.5, s32[1,256]{1,0:T(1,128)S(1)} %bitcast.3, f32[1,256]{1,0:T(1,128)S(1)} %bitcast.4, ...), custom_call_target="tpu_custom_call" | custom-call | tf_op jit(solution)/shard_map/pallas_call | solution.py:417
  143.1 0.7 copy.17
  143.8 0.7 copy.18
  144.5 0.7 copy.19
  145.2 0.7 copy.20
Async XLA Ops:
  0.6 0.7 copy-start.8
  0.6 0.7 copy-start.7
  0.7 0.7 copy-start.6
  1.3 0.7 copy-start.5
  2.0 1.0 copy-start
  2.9 1.0 copy-start.1
  3.9 1.0 copy-start.2
  4.9 0.9 copy-start.3
  5.8 0.9 copy-start.4

commit v2 on v1

v2 whole, which is shorter than its diff:
```python
import functools

import jax
import jax.numpy as jnp
from jax import lax
from jax.experimental import pallas as pl
from jax.experimental.pallas import tpu as pltpu
from jax.sharding import PartitionSpec as P

MESH = pl.DeviceIdType.MESH
bf16 = jnp.bfloat16
f32 = jnp.float32

beta_first = 0.9
beta_second = 0.95
adam_epsilon = 1e-08
learn_rate = 0.001
weight_decay = 0.1
bias_first = 1.0 - beta_first**10
bias_second = 1.0 - beta_second**10

LAG_SUM, LAG_ACT = 4, 8
AT_ONE, AT_TWO, AT_TURN = 8, 10, 13
CHUNKS = 4
CAP = 16
PARKS = ((0, 0), (0, 1), (2, 0))


def same_bytes(ref, sem):
    return pltpu.make_async_copy(ref, ref, sem)


def adamw_step(master, moment_one, moment_two, gradient):
    first_out = beta_first * moment_one + (1.0 - beta_first) * gradient
    second_out = beta_second * moment_two + (1.0 - beta_second) * gradient * gradient
    update = first_out / bias_first / (jnp.sqrt(second_out / bias_second) + adam_epsilon)
    master_out = master - learn_rate * (update + weight_decay * master)
    return master_out, first_out, second_out


def kernel(
    source_ref, *refs,
):
    inputs, outputs, scratch = refs[:8], refs[8:12], refs[12:]
    body(source_ref, inputs, *outputs, *scratch)


def body(
    source_ref, inputs,
    token_grad_ref, master_out_ref, first_out_ref, second_out_ref,
    place_ref, ids_ref, combine_ref, tokens_ref, out_grad_ref, master_ref, one_ref, two_ref,
    match, rows_out, rows_in, states, parked_0, parked_1, parked_2, onward, moved,
    weight, partial_gu, partial_dn, rs_gu, rs_dn, yb_gu, yb_dn, yr_gu, yr_dn, act_hid, act_gu, row_grad, returned, wgrad, turned, grads,
    in_sem, send_sem, rows_sem, park_sem, moved_sem, weight_sem, rs_sem, y_sem, ag_sem, ret_sem, turn_sem, grad_sem,
):
    p = lax.axis_index("dp")
    me = lax.axis_index("expert")
    s = lax.axis_index("shard")
    z, core = me // 2, me % 2
    x, yh = s // 2, s % 2
    n_owner = 32
    n_rows = n_owner * CAP
    chunk_rows = n_rows // CHUNKS
    block_rows = chunk_rows // 4
    width = tokens_ref.shape[1]
    ff = weight.shape[1]
    part_ff = ff // 8

    y = yh * 4 + p
    parked = (parked_0, parked_1, parked_2)
    staged = (place_ref, ids_ref, combine_ref, tokens_ref, out_grad_ref, master_ref, one_ref, two_ref)

    def load(i):
        return pltpu.make_async_copy(inputs[i], staged[i], in_sem.at[i])

    for i in (5, 0, 1, 2, 3, 4, 6, 7):
        load(i).start()

    def offset(n, i):
        rank = n - 1 - i
        return jnp.where(rank % 2 == 1, (rank + 1) // 2, (n - rank // 2) % n)

    barrier = pltpu.get_barrier_semaphore()

    def greet(device):
        pl.semaphore_signal(barrier, inc=1, device_id=device, device_id_type=MESH)

    def greet_owner(i, c):
        greet({"expert": (me + i) % n_owner})
        return c

    lax.fori_loop(1, n_owner, greet_owner, 0)
    for j in (1, 2, 3):
        greet({"shard": ((x + j) % 4) * 2 + yh})

    def greet_y(i, c):
        to = (y + i) % 8
        greet({"dp": to % 4, "shard": x * 2 + to // 4})
        return c

    lax.fori_loop(1, 8, greet_y, 0)
    diagonal = x == p

    def greet_spread(i, c):
        h, q = i // 4, i % 4

        @pl.when(jnp.logical_or(q != p, p * 2 + h != s))
        def _():
            greet({"dp": q, "shard": p * 2 + h})

        @pl.when(jnp.logical_or(x != p, i != s))
        def _():
            greet({"dp": x, "shard": i})

        return c

    lax.fori_loop(0, 8, greet_spread, 0)
    load(5).wait()
    states[0] = master_ref[0].astype(bf16)
    pl.semaphore_wait(barrier, jnp.where(diagonal, 55, 57))

    def is_park(a):
        shift, c = PARKS[a]
        zz = (z + 16 - shift) % 16
        return jnp.logical_and(core == c, zz % 4 != 3), jnp.minimum(zz - zz // 4, 11)

    def park(a):
        shift, to_core = PARKS[a]

        def step(i, c):
            to = (z + offset(16, i)) % 16
            place_in = (to + 16 - shift) % 16
            k = jnp.minimum(place_in - place_in // 4, 11)
            g, lane = k // 4, pl.multiple_of((k % 4) * 128, 128)
            dest = 2 * to + to_core
            holds_one = place_in % 4 != 3
            src = states.at[a, g, :, pl.ds(lane, 128)]

            @pl.when(jnp.logical_and(holds_one, dest != me))
            def _():
                pltpu.make_async_remote_copy(
                    src_ref=src, dst_ref=parked[a].at[me], send_sem=send_sem.at[a],
                    recv_sem=park_sem.at[a], device_id={"expert": dest}, device_id_type=MESH,
                ).start()

            @pl.when(jnp.logical_and(holds_one, dest == me))
            def _():
                pltpu.make_async_copy(src, parked[a].at[me], park_sem.at[a]).start()

            return c

        lax.fori_loop(0, 16, step, 0)

    def send_on(a):
        mine, k = is_park(a)
        g, lane = k // 4, pl.multiple_of((k % 4) * 128, 128)

        @pl.when(mine)
        def _():
            same_bytes(parked[a], park_sem.at[a]).wait()

            def step(i, c):
                o = ((z + offset(16, i // 2)) % 16) * 2 + i % 2
                onward[a, o] = parked[a][source_ref[o]]
                dst = moved.at[a, g, :, pl.ds(lane, 128)]

                @pl.when(o != me)
                def _():
                    pltpu.make_async_remote_copy(
                        src_ref=onward.at[a, o], dst_ref=dst, send_sem=send_sem.at[3 + a],
                        recv_sem=moved_sem.at[a], device_id={"expert": o}, device_id_type=MESH,
                    ).start()

                @pl.when(o == me)
                def _():
                    pltpu.make_async_copy(onward.at[a, o], dst, moved_sem.at[a]).start()

                return c

            lax.fori_loop(0, n_owner, step, 0)

    def states_sent(a):
        mine, _ = is_park(a)

        @pl.when(mine)
        def _():
            same_bytes(onward.at[a, pl.ds(0, 11)], send_sem.at[a]).wait()
            same_bytes(onward.at[a, pl.ds(0, 31)], send_sem.at[3 + a]).wait()

        @pl.when(jnp.logical_not(mine))
        def _():
            same_bytes(onward.at[a, pl.ds(0, 12)], send_sem.at[a]).wait()

    park(0)

    for i in range(5):
        load(i).wait()
    tok = tokens_ref.shape[0]
    eye = lax.broadcasted_iota(jnp.int32, (n_owner, n_owner), 0) == lax.broadcasted_iota(
        jnp.int32, (n_owner, n_owner), 1
    )
    place = jnp.sum(jnp.where(eye, place_ref[...].astype(f32), 0.0), axis=1, keepdims=True)
    onehot = jnp.where(
        lax.broadcasted_iota(jnp.int32, (n_owner, tok), 0) == ids_ref[...], 1.0, 0.0
    )
    before = jnp.where(
        lax.broadcasted_iota(jnp.int32, (tok, tok), 0) < lax.broadcasted_iota(jnp.int32, (tok, tok), 1),
        1.0, 0.0,
    ).astype(bf16)
    earlier = jnp.dot(onehot.astype(bf16), before, preferred_element_type=f32)
    position = jnp.sum(onehot * (earlier + place * float(CAP)), axis=0, keepdims=True)
    chosen = lax.broadcasted_iota(jnp.int32, (n_rows, tok), 0).astype(f32) == position
    match[...] = jnp.where(chosen, 1.0, 0.0).astype(bf16)
    scale = jnp.sum(jnp.where(chosen, combine_ref[...], 0.0), axis=1, keepdims=True)
    rows_out[:, :width] = jnp.dot(match[...], tokens_ref[...], preferred_element_type=f32).astype(bf16)
    rows_out[:, width:] = (
        scale * jnp.dot(match[...], out_grad_ref[...], preferred_element_type=f32)
    ).astype(bf16)

    send_on(0)

    def dispatch(i, c):
        rank, to_core = i // 2, i % 2
        dest = ((z + 16 - offset(16, rank)) % 16) * 2 + to_core
        src = rows_out.at[pl.ds(pl.multiple_of(dest * CAP, CAP), CAP), :]
        dst = rows_in.at[pl.ds(pl.multiple_of((rank * 2 + core) * CAP, CAP), CAP), :]
        sem = rows_sem.at[rank // (16 // CHUNKS)]

        @pl.when(dest != me)
        def _():
            pltpu.make_async_remote_copy(
                src_ref=src, dst_ref=dst, send_sem=send_sem.at[6], recv_sem=sem,
                device_id={"expert": dest}, device_id_type=MESH,
            ).start()

        @pl.when(dest == me)
        def _():
            pltpu.make_async_copy(src, dst, sem).start()

        return c

    lax.fori_loop(0, n_owner, dispatch, 0)

    same_bytes(moved.at[0], moved_sem.at[0]).wait()

    def spread_part(part, i, c):
        to = (y + offset(8, i)) % 8
        h, q = to // 4, to % 4
        mats = pl.ds(0, 2) if part == 0 else pl.ds(2, 1)
        src = moved.at[0, mats, :, pl.ds(pl.multiple_of(h * width, width), width)]
        dst = weight.at[mats, pl.ds(pl.multiple_of(s * part_ff, 16), part_ff), :]
        away = jnp.logical_or(q != p, p * 2 + h != s)

        @pl.when(away)
        def _():
            pltpu.make_async_remote_copy(
                src_ref=src, dst_ref=dst, send_sem=send_sem.at[7], recv_sem=weight_sem.at[part],
                device_id={"dp": q, "shard": p * 2 + h}, device_id_type=MESH,
            ).start()

        @pl.when(jnp.logical_not(away))
        def _():
            pltpu.make_async_copy(src, dst, weight_sem.at[part]).start()

        return c

    lax.fori_loop(0, 8, functools.partial(spread_part, 0), 0)
    lax.fori_loop(0, 8, functools.partial(spread_part, 1), 0)
    load(6).wait()
    states[1] = one_ref[0].astype(bf16)
    park(1)
    load(7).wait()
    states[2] = two_ref[0].astype(bf16)
    park(2)
    same_bytes(weight.at[pl.ds(0, 2)], weight_sem.at[0]).wait()

    nt = (((1,), (1,)), ((), ()))

    def own_rows(c):
        return pl.ds(pl.multiple_of(c * chunk_rows + x * block_rows, 16), block_rows)

    sides = (
        (partial_gu, rs_gu, yb_gu, yr_gu, act_hid, rs_dn),
        (partial_dn, rs_dn, yb_dn, yr_dn, act_gu, rs_gu),
    )

    def products(part, c):
        partial, rs = sides[part][:2]
        unit = part * CHUNKS + c
        here = pl.ds(c * chunk_rows, chunk_rows)
        if part == 0:
            same_bytes(rows_in.at[here], rows_sem.at[c]).wait()
            for g in range(2):
                partial[here, g * ff : (g + 1) * ff] = lax.dot_general(
                    rows_in[here, :width], weight[g], nt, preferred_element_type=f32
                ).astype(bf16)
        else:
            partial[here, :] = lax.dot_general(
                rows_in[here, width:], weight[2], nt, preferred_element_type=f32
            ).astype(bf16)
        for j in (2, 1, 3):
            xx = (x + j) % 4
            pltpu.make_async_remote_copy(
                src_ref=partial.at[pl.ds(pl.multiple_of(c * chunk_rows + xx * block_rows, 16), block_rows), :],
                dst_ref=rs.at[c, j - 1], send_sem=send_sem.at[8 + part], recv_sem=rs_sem.at[unit],
                device_id={"shard": xx * 2 + yh}, device_id_type=MESH,
            ).start()

    def half_sums(part, c):
        partial, rs, yb, yr = sides[part][:4]
        unit = part * CHUNKS + c
        same_bytes(rs.at[c], rs_sem.at[unit]).wait()
        total = partial[own_rows(c), :].astype(f32)
        for j in range(3):
            total += rs[c, j].astype(f32)
        yb[c] = total.astype(bf16)
        pltpu.make_async_remote_copy(
            src_ref=yb.at[c], dst_ref=yr.at[c], send_sem=send_sem.at[10 + part], recv_sem=y_sem.at[unit],
            device_id={"shard": x * 2 + 1 - yh}, device_id_type=MESH,
        ).start()

    def activations(part, c):
        act, yb, yr = sides[part][4], sides[part][2], sides[part][3]
        unit = part * CHUNKS + c
        same_bytes(yr.at[c], y_sem.at[unit]).wait()
        gate_up = yb_gu[c].astype(f32) + yr_gu[c].astype(f32)
        gate, up = gate_up[:, :ff], gate_up[:, ff:]
        sigma = jax.nn.sigmoid(gate)
        active = gate * sigma
        here = own_rows(c)
        if part == 0:
            act[here, :] = (active * up).astype(bf16)
        else:
            grad_hidden = yb[c].astype(f32) + yr[c].astype(f32)
            act[here, :ff] = (grad_hidden * up * sigma * (1.0 + gate * (1.0 - sigma))).astype(bf16)
            act[here, ff:] = (grad_hidden * active).astype(bf16)
        for j in (2, 1, 3):
            xx = (x + j) % 4
            pltpu.make_async_remote_copy(
                src_ref=act.at[here, :], dst_ref=act.at[here, :], send_sem=send_sem.at[12 + part],
                recv_sem=ag_sem.at[unit], device_id={"shard": xx * 2 + yh}, device_id_type=MESH,
            ).start()

    def gathered(part, c):
        same_bytes(sides[part][5].at[c], ag_sem.at[part * CHUNKS + c]).wait()

    def row_grads(c):
        here = pl.ds(c * chunk_rows, chunk_rows)
        row_grad[here, :] = (
            jnp.dot(act_gu[here, :ff], weight[0], preferred_element_type=f32)
            + jnp.dot(act_gu[here, ff:], weight[1], preferred_element_type=f32)
        ).astype(bf16)

        def give_back(i, carry):
            rank, to_core = i // 2, i % 2
            dest = ((z + offset(16, rank)) % 16) * 2 + to_core
            src = row_grad.at[pl.ds(pl.multiple_of(i * CAP, CAP), CAP), :]
            dst = returned.at[pl.ds(pl.multiple_of(me * CAP, CAP), CAP), :]

            @pl.when(dest != me)
            def _():
                pltpu.make_async_remote_copy(
                    src_ref=src, dst_ref=dst, send_sem=send_sem.at[14], recv_sem=ret_sem,
                    device_id={"expert": dest}, device_id_type=MESH,
                ).start()

            @pl.when(dest == me)
            def _():
                pltpu.make_async_copy(src, dst, ret_sem).start()

            return carry

        lax.fori_loop(c * (n_owner // CHUNKS), (c + 1) * (n_owner // CHUNKS), give_back, 0)

    tn = (((0,), (0,)), ((), ()))
    pair_ff = 2 * part_ff

    def along_x(g):
        left, right = (
            (act_gu[:, g * ff : (g + 1) * ff], rows_in[:, :width])
            if g < 2
            else (act_hid[...], rows_in[:, width:])
        )
        wgrad[g] = lax.dot_general(left, right, tn, preferred_element_type=f32).astype(bf16)
        for j in (2, 1, 3):
            xx = (x + j) % 4
            pltpu.make_async_remote_copy(
                src_ref=wgrad.at[g, pl.ds(pl.multiple_of(xx * pair_ff, 16), pair_ff), :],
                dst_ref=turned.at[g, x], send_sem=send_sem.at[15], recv_sem=turn_sem.at[g],
                device_id={"shard": xx * 2 + yh}, device_id_type=MESH,
            ).start()
        pltpu.make_async_copy(
            wgrad.at[g, pl.ds(pl.multiple_of(x * pair_ff, 16), pair_ff), :], turned.at[g, x], turn_sem.at[g]
        ).start()

    def along_y(g):
        same_bytes(turned.at[g], turn_sem.at[g]).wait()

        def to_holder(i, c):
            to = (y + offset(8, i)) % 8
            h, q = to // 4, to % 4
            src = turned.at[g, q, pl.ds(pl.multiple_of(h * part_ff, 16), part_ff), :]
            dst = grads.at[g, y]

            @pl.when(to != y)
            def _():
                pltpu.make_async_remote_copy(
                    src_ref=src, dst_ref=dst, send_sem=send_sem.at[16], recv_sem=grad_sem.at[g],
                    device_id={"dp": q, "shard": x * 2 + h}, device_id_type=MESH,
                ).start()

            @pl.when(to == y)
            def _():
                pltpu.make_async_copy(src, dst, grad_sem.at[g]).start()

            return c

        lax.fori_loop(0, 8, to_holder, 0)

    units = [(part, c) for part in range(2) for c in range(CHUNKS)]
    for step in range(len(units) + LAG_ACT):
        if step == CHUNKS:
            same_bytes(weight.at[pl.ds(2, 1)], weight_sem.at[1]).wait()
        if step < len(units):
            products(*units[step])
        if 0 <= step - LAG_SUM < len(units):
            half_sums(*units[step - LAG_SUM])
        if 0 <= step - LAG_ACT:
            activations(*units[step - LAG_ACT])
        if step == AT_ONE:
            send_on(1)
        if step == AT_TURN:
            for c in range(CHUNKS):
                gathered(0, c)
            along_x(2)
        if step == AT_TWO:
            send_on(2)
    along_y(2)
    for c in range(CHUNKS - 1):
        gathered(1, c)
        row_grads(c)
    gathered(1, CHUNKS - 1)
    along_x(0)
    along_x(1)
    row_grads(CHUNKS - 1)
    along_y(0)
    along_y(1)

    same_bytes(returned, ret_sem).wait()
    token_grad_ref[...] = lax.dot_general(
        match[...], returned[...], tn, preferred_element_type=f32
    ).astype(bf16)

    same_bytes(moved.at[1], moved_sem.at[1]).wait()
    same_bytes(moved.at[2], moved_sem.at[2]).wait()
    for g in (2, 0, 1):
        same_bytes(grads.at[g], grad_sem.at[g]).wait()
        for h in range(2):
            half = slice(h * width, (h + 1) * width)
            gradient = grads[g, h * 4].astype(f32)
            for q in range(1, 4):
                gradient += grads[g, h * 4 + q].astype(f32)
            a, b, d = adamw_step(
                moved[0, g, :, half].astype(f32), moved[1, g, :, half].astype(f32),
                moved[2, g, :, half].astype(f32), gradient,
            )
            master_out_ref[0, g, :, half] = a
            first_out_ref[0, g, :, half] = b
            second_out_ref[0, g, :, half] = d

    for a in range(3):
        states_sent(a)
    same_bytes(rows_out.at[pl.ds(0, 31 * CAP)], send_sem.at[6]).wait()

    @pl.when(diagonal)
    def _():
        same_bytes(wgrad.at[:, pl.ds(0, 7 * part_ff), :], send_sem.at[7]).wait()

    @pl.when(jnp.logical_not(diagonal))
    def _():
        same_bytes(wgrad, send_sem.at[7]).wait()

    same_bytes(turned.at[:, pl.ds(0, 3)], send_sem.at[15]).wait()
    same_bytes(grads.at[:, pl.ds(0, 7)], send_sem.at[16]).wait()
    for part in range(2):
        same_bytes(sides[part][1], send_sem.at[8 + part]).wait()
        same_bytes(sides[part][2], send_sem.at[10 + part]).wait()
        same_bytes(sides[part][5], send_sem.at[12 + part]).wait()
    same_bytes(row_grad.at[pl.ds(0, 31 * CAP)], send_sem.at[14]).wait()


def on_device(
    tokens, out_grad, expert_ids, combine, old_place, new_place, master, moment_one, moment_two
):
    n_owner = 32
    owners = jnp.arange(n_owner, dtype=jnp.int32)
    holds = (new_place[:, None] == owners[None, :]).astype(jnp.int32)
    source_owner = jnp.sum(old_place[:, None] * holds, axis=0)
    tok, width = tokens.shape
    _, mats, part_ff, held_width = master.shape
    ff = part_ff * 8
    rows = n_owner * CAP
    block = rows // CHUNKS // 4
    vmem = pl.BlockSpec(memory_space=pltpu.VMEM)
    dma = pltpu.SemaphoreType.DMA
    return pl.pallas_call(
        kernel,
        out_shape=(
            jax.ShapeDtypeStruct(tokens.shape, bf16),
            jax.ShapeDtypeStruct(master.shape, f32),
            jax.ShapeDtypeStruct(master.shape, f32),
            jax.ShapeDtypeStruct(master.shape, f32),
        ),
        in_specs=[pl.BlockSpec(memory_space=pltpu.SMEM)] + [pl.BlockSpec(memory_space=pltpu.HBM)] * 8,
        out_specs=(vmem,) * 4,
        scratch_shapes=[
            pltpu.VMEM((1, n_owner), jnp.int32),
            pltpu.VMEM((1, tok), jnp.int32),
            pltpu.VMEM((1, tok), f32),
            pltpu.VMEM(tokens.shape, bf16),
            pltpu.VMEM(tokens.shape, bf16),
            pltpu.VMEM(master.shape, f32),
            pltpu.VMEM(master.shape, f32),
            pltpu.VMEM(master.shape, f32),
            pltpu.VMEM((rows, tok), bf16),
            pltpu.VMEM((rows, 2 * width), bf16),
            pltpu.VMEM((rows, 2 * width), bf16),
            pltpu.VMEM((3, mats, part_ff, held_width), bf16),
            pltpu.VMEM((n_owner, part_ff, 128), bf16),
            pltpu.VMEM((n_owner, part_ff, 128), bf16),
            pltpu.VMEM((n_owner, part_ff, 128), bf16),
            pltpu.VMEM((3, n_owner, part_ff, 128), bf16),
            pltpu.VMEM((3, mats, part_ff, held_width), bf16),
            pltpu.VMEM((mats, ff, width), bf16),
            pltpu.VMEM((rows, 2 * ff), bf16),
            pltpu.VMEM((rows, ff), bf16),
            pltpu.VMEM((CHUNKS, 3, block, 2 * ff), bf16),
            pltpu.VMEM((CHUNKS, 3, block, ff), bf16),
            pltpu.VMEM((CHUNKS, block, 2 * ff), bf16),
            pltpu.VMEM((CHUNKS, block, ff), bf16),
            pltpu.VMEM((CHUNKS, block, 2 * ff), bf16),
            pltpu.VMEM((CHUNKS, block, ff), bf16),
            pltpu.VMEM((rows, ff), bf16),
            pltpu.VMEM((rows, 2 * ff), bf16),
            pltpu.VMEM((rows, width), bf16),
            pltpu.VMEM((rows, width), bf16),
            pltpu.VMEM((mats, ff, width), bf16),
            pltpu.VMEM((mats, 4, 2 * part_ff, width), bf16),
            pltpu.VMEM((mats, 8, part_ff, width), bf16),
            dma((8,)),
            dma((17,)),
            dma((CHUNKS,)),
            dma((3,)),
            dma((3,)),
            dma((2,)),
            dma((2 * CHUNKS,)),
            dma((2 * CHUNKS,)),
            dma((2 * CHUNKS,)),
            dma,
            dma((3,)),
            dma((3,)),
        ],
        compiler_params=pltpu.CompilerParams(
            collective_id=0, has_side_effects=True, vmem_limit_bytes=60 * 1024 * 1024
        ),
    )(
        source_owner, new_place.reshape(1, n_owner), expert_ids.reshape(1, tok),
        combine.reshape(1, tok), tokens, out_grad, master, moment_one, moment_two,
    )


def solution(mesh):
    in_specs = (
        P(("dp", "expert"), "shard"),
        P(("dp", "expert"), "shard"),
        P(("dp", "expert"), None),
        P(("dp", "expert"), None),
        P(),
        P(),
        P("expert", None, "shard", "dp"),
        P("expert", None, "shard", "dp"),
        P("expert", None, "shard", "dp"),
    )
    out_specs = (
        P(("dp", "expert"), "shard"),
        P("expert", None, "shard", "dp"),
        P("expert", None, "shard", "dp"),
        P("expert", None, "shard", "dp"),
    )
    return jax.shard_map(
        on_device, mesh=mesh, in_specs=in_specs, out_specs=out_specs, check_vma=False
    )
```

time: 146 us -> 122 us (0.84)
  the two profiles are of different devices: /device:TPU:61 before, /device:TPU:64 now
where the time goes in v2:
time: 122 us; the launch traced here: 121 us
  Pallas kernels  114 us (93%)
  local copies, waits for them, and re-layouts  5.75 us (5%)
    pallas_call x1, Pallas kernels, on_device(): pl.pallas_call(kernel, out_shape=(jax.ShapeDtypeStruct(tokens.shape, bf16...  114 us
    unnamed x12, local copies, waits for them, and re-layouts  5.75 us

profile of v2, /device:TPU:64, one launch (start us, length us, event | category | flops | bytes accessed | tf_op | source)
XLA Modules:
  0.0 121.3 jit_solution(5061246870468831969)
XLA Ops:
  0.6 0.0 copy-start.2
  0.6 0.0 copy-start.3
  0.7 0.6 copy-done.2
  1.3 0.0 copy-done.3
  1.3 0.6 select_reduce_fusion.source_ref
  1.9 114.3 %shard_map.120 = (bf16[256,256]{1,0:T(8,128)(2,1)}, f32[1,3,48,512]{3,2,1,0:T(8,128)}, f32[1,3,48,512]{3,2,1,0:T(8,128)}, f32[1,3,48,512]{3,2,1,0:T(8,128)}) custom-call(s32[32]{0:T(128)} %select_reduce_fusion.source_ref, s32[1,32]{1,0:T(1,128)} %bitcast.5, s32[1,256]{1,0:T(1,128)} %bitcast.3, f32[1,256]{1,0:T(1,128)} %bitcast.4, bf16[256,256]{1,0:T(8,128)(2,1)} %refs_3_.1, ...), custom_call_target="tpu_custom_call" | custom-call | tf_op jit(solution)/shard_map/pallas_call | solution.py:506
  116.2 1.6 %copy.17 = bf16[256,256]{1,0:T(8,128)(2,1)} copy(bf16[256,256]{1,0:T(8,128)(2,1)} %get-tuple-element.8) | data formatting | bytes 262144
  117.8 0.0 copy-start.1
  117.8 1.7 %copy.18 = f32[1,3,48,512]{3,2,1,0:T(8,128)} copy(f32[1,3,48,512]{3,2,1,0:T(8,128)} %get-tuple-element.9) | data formatting | bytes 589824
  119.5 0.0 copy-done.1
  119.6 0.0 copy-start
  119.6 0.7 copy.19
  120.3 0.4 copy-done
  120.6 0.7 copy.20
Async XLA Ops:
  0.6 0.7 copy-start.2
  0.6 0.7 copy-start.3
  117.8 1.7 %copy-start.1 = (f32[1,3,48,512]{3,2,1,0:T(8,128)S(1)}, f32[1,3,48,512]{3,2,1,0:T(8,128)}, u32[]{:S(2)}) copy-start(f32[1,3,48,512]{3,2,1,0:T(8,128)} %get-tuple-element.10) | copy-start | bytes 884740
  119.6 1.1 copy-start

commit v3 on v2

--- a/solution.py
+++ b/solution.py
@@ -20,7 +20,7 @@
 bias_second = 1.0 - beta_second**10
 
 LAG_SUM, LAG_ACT = 4, 8
-AT_ONE, AT_TWO, AT_TURN = 8, 10, 13
+AT_ONE, AT_TWO, AT_TURN = 8, 10, 12
 CHUNKS = 4
 CAP = 16
 PARKS = ((0, 0), (0, 1), (2, 0))
@@ -446,11 +446,6 @@
     along_y(0)
     along_y(1)
 
-    same_bytes(returned, ret_sem).wait()
-    token_grad_ref[...] = lax.dot_general(
-        match[...], returned[...], tn, preferred_element_type=f32
-    ).astype(bf16)
-
     same_bytes(moved.at[1], moved_sem.at[1]).wait()
     same_bytes(moved.at[2], moved_sem.at[2]).wait()
     for g in (2, 0, 1):
@@ -467,6 +462,11 @@
             master_out_ref[0, g, :, half] = a
             first_out_ref[0, g, :, half] = b
             second_out_ref[0, g, :, half] = d
+
+    same_bytes(returned, ret_sem).wait()
+    token_grad_ref[...] = lax.dot_general(
+        match[...], returned[...], tn, preferred_element_type=f32
+    ).astype(bf16)
 
     for a in range(3):
         states_sent(a)

time: 122 us -> 121 us (level)
  no operation moved by 1% of the time
where the time goes in v3:
time: 121 us
  Pallas kernels  114 us (94%)
  local copies, waits for them, and re-layouts  5.75 us (5%)
    pallas_call x1, Pallas kernels, on_device(): pl.pallas_call(kernel, out_shape=(jax.ShapeDtypeStruct(tokens.shape, bf16...  114 us
    unnamed x12, local copies, waits for them, and re-layouts  5.75 us

profile of v3, /device:TPU:64, one launch (start us, length us, event | category | flops | bytes accessed | tf_op | source)
XLA Modules:
  0.0 120.9 jit_solution(13664455890290489762)
XLA Ops:
  0.6 0.0 copy-start.2
  0.6 0.0 copy-start.3
  0.7 0.6 copy-done.2
  1.3 0.0 copy-done.3
  1.3 0.6 select_reduce_fusion.source_ref
  1.9 113.9 %shard_map.120 = (bf16[256,256]{1,0:T(8,128)(2,1)}, f32[1,3,48,512]{3,2,1,0:T(8,128)}, f32[1,3,48,512]{3,2,1,0:T(8,128)}, f32[1,3,48,512]{3,2,1,0:T(8,128)}) custom-call(s32[32]{0:T(128)} %select_reduce_fusion.source_ref, s32[1,32]{1,0:T(1,128)} %bitcast.5, s32[1,256]{1,0:T(1,128)} %bitcast.3, f32[1,256]{1,0:T(1,128)} %bitcast.4, bf16[256,256]{1,0:T(8,128)(2,1)} %refs_3_.1, ...), custom_call_target="tpu_custom_call" | custom-call | tf_op jit(solution)/shard_map/pallas_call | solution.py:506
  115.8 1.6 %copy.17 = bf16[256,256]{1,0:T(8,128)(2,1)} copy(bf16[256,256]{1,0:T(8,128)(2,1)} %get-tuple-element.8) | data formatting | bytes 262144
  117.4 0.0 copy-start.1
  117.4 1.7 %copy.18 = f32[1,3,48,512]{3,2,1,0:T(8,128)} copy(f32[1,3,48,512]{3,2,1,0:T(8,128)} %get-tuple-element.9) | data formatting | bytes 589824
  119.1 0.0 copy-done.1
  119.1 0.0 copy-start
  119.1 0.7 copy.19
  119.9 0.4 copy-done
  120.2 0.7 copy.20
Async XLA Ops:
  0.6 0.7 copy-start.2
  0.6 0.7 copy-start.3
  117.4 1.7 %copy-start.1 = (f32[1,3,48,512]{3,2,1,0:T(8,128)S(1)}, f32[1,3,48,512]{3,2,1,0:T(8,128)}, u32[]{:S(2)}) copy-start(f32[1,3,48,512]{3,2,1,0:T(8,128)} %get-tuple-element.10) | copy-start | bytes 884740
  119.1 1.1 copy-start
